TPU v7x, 512 devices: a whole 4x8x8 slice. The times are simulated.
512 devices in a mesh: inst: 16 (over y, core), tp: 32 (over z, x).
Axes of the slice: x: 4, y: 8, z: 8, core: 2. Of those that a mesh axis runs over, the one named last changes fastest.
Arguments:
- queries: bfloat16 [256, 8192], P('inst', 'tp'), may hold values from -5 to 5
- home_kv: bfloat16 [384, 32, 128, 256], P('inst', 'tp'), may hold values from -5 to 5, as said below
- lent_kv: bfloat16 [256, 32, 128, 256], P('inst', 'tp'), may hold values from -5 to 5, as said below
- page_table: int32 [256, 2], P('inst'), may hold values from -1 to 23, as said below
- borrowed: int32 [256, 2], P('inst'), may hold values from -1 to 255, as said below
- lengths: int32 [256], P('inst'), may hold values from 1 to 512, as said below
- out_weight: bfloat16 [8192, 4096], P('tp'), may hold values from -0.25 to 0.25
Outputs:
- projected: bfloat16 [256, 4096], P('inst', 'tp')
Inputs may be any that keep to these rules, and one draw needn't show every extreme that they name: `page_table`: row r lists the home pages of request r in sequence order by their number within its instance's 24 pages, then -1 where it has fewer than 2; every request has one or more, and each page of an instance is listed exactly once. `borrowed`: row r lists the pages that request r holds after its home pages, in sequence order, as the lending instance times 16 plus the slot, then -1; each of the 256 lent slots is listed exactly once, and a slot may lie in the request's own instance. `lengths`: with p the number of entries of the request in page_table and borrowed other than -1, the length is above 128 * (p - 1) and at most 128 * p. `home_kv`: the copies of one key-value head along dimension 1 are equal. `lent_kv`: the copies of one key-value head along dimension 1 are equal.
All inputs are finite; a program needn't handle non-finite values.
Results may differ from a plain program's by a relative error of at most 0.0085.
Values may be sent and summed in bfloat16 or wider, within the bound.
A program may use at most 64 MiB of HBM per device.

v0:
```python
import math

import jax
import jax.numpy as jnp
from jax import lax
from jax.sharding import PartitionSpec as P

HD = 128
PAGE = 128
HOME_MOST = 2
BORROW_MOST = 2


sentinel = -1e30


def page_stats(scores, usable):
    masked = jnp.where(usable, scores, sentinel)
    maxima = jnp.max(masked, axis=-1)
    weights = jnp.where(usable, jnp.exp(masked - maxima[..., None]), 0.0)
    rounded = weights.astype(jnp.bfloat16)
    totals = jnp.sum(rounded.astype(jnp.float32), axis=-1)
    return (maxima, totals, rounded)


def shards(queries, home_kv, lent_kv, page_table, borrowed, lengths, out_weight):
    req_local = queries.shape[0]
    heads_dev = queries.shape[1] // HD
    lent_slots = lent_kv.shape[0]
    score_scale = 1.0 / math.sqrt(HD)
    inst_count = lax.axis_size("inst")
    home_count = jnp.sum((page_table >= 0).astype(jnp.int32), axis=1)
    remainder = lengths - home_count * PAGE
    borrow_all, remain_all = (
        lax.all_gather(borrowed, "inst", axis=0, tiled=True),
        lax.all_gather(remainder, "inst", axis=0, tiled=True),
    )
    query_all = lax.all_gather(queries, "inst", axis=0, tiled=True)
    home_slots = home_kv[:, 0]
    home_pages = home_slots[jnp.maximum(page_table, 0)]
    query_heads = queries.reshape(req_local, heads_dev, HD)
    home_scores = (
        jnp.einsum(
            "rgd,rptd->rpgt", query_heads, home_pages[..., :HD], preferred_element_type=jnp.float32
        )
        * score_scale
    )
    page_order = jnp.arange(HOME_MOST, dtype=jnp.int32)
    token_order = jnp.arange(PAGE, dtype=jnp.int32)
    positions = page_order[:, None] * PAGE + token_order[None, :]
    home_usable = (page_order[None, :, None] < home_count[:, None, None]) & (
        positions[None] < lengths[:, None, None]
    )
    home_max, home_tot, home_wts = page_stats(home_scores, home_usable[:, :, None, :])
    home_part = jnp.einsum(
        "rpgt,rptd->rpgd", home_wts, home_pages[..., HD:], preferred_element_type=jnp.float32
    )
    home_peak = jnp.max(home_max, axis=1)
    home_factor = jnp.exp(home_max - home_peak[:, None])
    home_weight = jnp.maximum(jnp.sum(home_factor * home_tot, axis=1), 1.0)
    home_out = jnp.sum(home_factor[..., None] * home_part, axis=1) / home_weight[..., None]
    home_out = lax.optimization_barrier(home_out.astype(jnp.bfloat16)).astype(jnp.float32)
    home_lse = home_peak + jnp.log(home_weight)
    entries = borrow_all.reshape(-1)
    entry_order = jnp.arange(entries.shape[0], dtype=jnp.int32)
    slot_global = lax.axis_index("inst") * lent_slots + jnp.arange(lent_slots, dtype=jnp.int32)
    matches = (entries[:, None] == slot_global[None, :]).astype(jnp.int32)
    owner_req = jnp.sum(matches * (entry_order // BORROW_MOST)[:, None], axis=0)
    page_rank = jnp.sum(matches * (entry_order % BORROW_MOST)[:, None], axis=0)
    occupied = jnp.sum(matches, axis=0) > 0
    slot_queries = query_all[owner_req].reshape(lent_slots, heads_dev, HD)
    slot_remain = remain_all[owner_req]
    slot_pages = lent_kv[:, 0]
    lent_scores = (
        jnp.einsum(
            "sgd,std->sgt", slot_queries, slot_pages[..., :HD], preferred_element_type=jnp.float32
        )
        * score_scale
    )
    lent_usable = occupied[:, None] & (
        page_rank[:, None] * PAGE + token_order[None, :] < slot_remain[:, None]
    )
    lent_max, lent_tot, lent_wts = page_stats(lent_scores, lent_usable[:, None, :])
    lent_part = jnp.einsum(
        "sgt,std->sgd", lent_wts, slot_pages[..., HD:], preferred_element_type=jnp.float32
    )
    request_total = query_all.shape[0]
    member_mask = (
        owner_req[None, :] == jnp.arange(request_total, dtype=jnp.int32)[:, None]
    ) & occupied[None, :]
    lend_peak = jnp.max(jnp.where(member_mask[:, :, None], lent_max[None], sentinel), axis=1)
    slot_factor = jnp.where(
        occupied[:, None],
        jnp.exp(jnp.where(occupied[:, None], lent_max - lend_peak[owner_req], 0.0)),
        0.0,
    )
    member_ones = member_mask.astype(jnp.float32)
    lend_weight = jnp.maximum(
        jnp.dot(member_ones, slot_factor * lent_tot, precision=lax.Precision.HIGHEST), 1.0
    )
    lend_sum = jnp.einsum(
        "rs,sgd->rgd",
        member_ones,
        slot_factor[..., None] * lent_part,
        precision=lax.Precision.HIGHEST,
    )
    lend_out = lax.optimization_barrier(
        (lend_sum / lend_weight[..., None]).astype(jnp.bfloat16)
    ).astype(jnp.float32)
    lend_lse = lend_peak + jnp.log(lend_weight)
    sent_out = lend_out.reshape(inst_count, req_local, heads_dev * HD)
    sent_lse = lend_lse.reshape(inst_count, req_local, heads_dev)
    back_out, back_lse = (
        lax.all_to_all(sent_out, "inst", split_axis=0, concat_axis=0, tiled=True),
        lax.all_to_all(sent_lse, "inst", split_axis=0, concat_axis=0, tiled=True),
    )
    summit = jnp.maximum(jnp.max(back_lse, axis=0), home_lse)
    shares = jnp.exp(back_lse - summit[None])
    home_share = jnp.exp(home_lse - summit)
    numerator = (
        jnp.sum(shares[..., None] * back_out.reshape(inst_count, req_local, heads_dev, HD), axis=0)
        + home_share[..., None] * home_out
    )
    denominator = jnp.sum(shares, axis=0) + home_share
    attended = (
        (numerator / denominator[..., None]).astype(jnp.bfloat16).reshape(req_local, heads_dev * HD)
    )
    partial_proj = jnp.dot(attended, out_weight, preferred_element_type=jnp.float32)
    return lax.psum_scatter(partial_proj, "tp", scatter_dimension=1, tiled=True).astype(
        jnp.bfloat16
    )


def solution(mesh):
    placed = (
        P("inst", "tp"),
        P("inst", "tp", None, None),
        P("inst", "tp", None, None),
        P("inst", None),
        P("inst", None),
        P("inst"),
        P("tp", None),
    )
    return jax.shard_map(
        shards, mesh=mesh, in_specs=placed, out_specs=P("inst", "tp"), check_vma=False
    )
```

profile of v0, /device:TPU:1, one launch (start us, length us, event | category | flops | bytes accessed | tf_op | source)
XLA Modules:
  0.0 298.0 jit_solution(8156980571540144569)
XLA Ops:
  6.6 21.2 %all-gather = s32[16,16,2]{1,2,0:T(2,128)S(1)} all-gather(s32[1,16,2]{1,2,0:T(2,128)} %bitcast.33), channel_id=1, replica_groups=mesh['inst'=16,'tp'=32] {'inst'}, dimensions={0}, use_global_device_ids=true | all-gather | bytes 2176 | tf_op jit(solution)/shard_map/all_gather | solution.py:35
  27.8 0.2 copy.50
  28.1 0.2 fusion.10
  28.4 0.7 broadcast_maximum_fusion.1
  29.1 1.3 dynamic-slice
  31.0 0.8 subtract_dynamic-update-slice_fusion
  31.8 9.8 %all-reduce = s32[256]{0:T(256)S(1)} all-reduce(s32[256]{0:T(256)S(1)} %subtract_dynamic-update-slice_fusion), channel_id=1, replica_groups=mesh['inst'=16,'tp'=32] {'inst'}, use_global_device_ids=true, to_apply=%add | all-reduce | flops 256 | bytes 2048
  41.5 19.4 %all_gather.11 = bf16[256,256]{1,0:T(8,128)(2,1)S(1)} all-gather(bf16[16,256]{1,0:T(8,128)(2,1)} %param.7), channel_id=1, replica_groups=mesh['inst'=16,'tp'=32] {'inst'}, dimensions={0}, use_global_device_ids=true | all-gather | bytes 139264 | tf_op jit(solution)/shard_map/all_gather | solution.py:38
  60.9 0.7 gather_fusion
  61.6 0.6 gather_fusion.1
  62.4 1.5 fusion.37
  64.2 0.6 gather_fusion.2
  64.8 0.2 convert_reduce_fusion.1
  65.0 0.2 log_add_fusion
  65.3 0.6 copy.53
  65.9 3.5 %all-to-all-start = ((f32[16,16,2]{1,2,0:T(2,128)}), f32[16,16,2]{1,2,0:T(2,128)S(1)}, u32[]{:S(2)}, u32[]{:S(2)}) async-start(f32[16,16,2]{1,2,0:T(2,128)} %copy.53), calls=%async_computation | async-start | bytes 32768 | tf_op jit(solution)/shard_map/all_to_all | solution.py:115
  69.8 0.2 convolution_multiply_fusion.2
  70.1 3.4 %gather_fusion.3 = bf16[32,128,256]{2,1,0:T(8,128)(2,1)} fusion(bf16[24,128,256]{2,1,0:T(8,128)(2,1)} %bitcast.29, s32[1024]{0:T(1024)S(1)} %pad_clamp_fusion), kind=kCustom, calls=%fused_computation.3 | custom fusion | bytes 4194432 | tf_op jit(solution)/shard_map/gather | solution.py:40
  73.6 1.8 fusion.34
  75.4 0.2 convert_reduce_fusion
  75.7 0.4 fusion
  76.1 0.4 fusion.3
  76.6 0.1 copy.59
  76.8 0.9 reshape.281
  77.7 7.3 %all-to-all-start.1 = ((f32[16,16,256]{2,1,0:T(8,128)}), f32[16,16,256]{2,1,0:T(8,128)S(1)}, u32[]{:S(2)}, u32[]{:S(2)}) async-start(f32[16,16,256]{2,1,0:T(8,128)} %reshape.281), calls=%async_computation.1 | async-start | bytes 524288 | tf_op jit(solution)/shard_map/all_to_all | solution.py:114
  85.5 0.2 copy.57
  85.6 0.3 mul.106
  86.0 0.2 mul.107
  86.2 10.5 %all-to-all-done.1 = f32[16,16,256]{2,1,0:T(8,128)S(1)} async-done(((f32[16,16,256]{2,1,0:T(8,128)}), f32[16,16,256]{2,1,0:T(8,128)S(1)}, u32[]{:S(2)}, u32[]{:S(2)}) %all-to-all-start.1) | async-done | bytes 262176 | tf_op jit(solution)/shard_map/all_to_all | solution.py:114
  96.9 1.1 fusion.16
  98.0 191.8 %reduce-scatter.2.cloned.1.call-done = f32[16,128]{1,0:T(8,128)} async-done(((f32[16,4096]{1,0:T(8,128)}), f32[16,128]{1,0:T(8,128)}) %reduce-scatter.2.cloned.1.call-update) | async-done | bytes 8208 | tf_op jit(solution)/shard_map/reduce_scatter | solution.py:129
  289.8 1.3 convert_element_type.45
  (51 shorter events, 2.1 us)
Async XLA Ops:
  6.5 90.3 %copy-start = (bf16[256,4096]{1,0:T(8,128)(2,1)S(1)}, bf16[256,4096]{1,0:T(8,128)(2,1)}, u32[]{:S(2)}) copy-start(bf16[256,4096]{1,0:T(8,128)(2,1)} %param.13) | copy-start | bytes 6291460
  6.5 63.5 %copy-start.3 = (s32[16]{0:T(128)S(1)}, s32[16]{0:T(128)}, u32[]{:S(2)}) copy-start(s32[16]{0:T(128)} %param.12) | copy-start | bytes 196
  6.5 62.9 %copy-start.2 = (bf16[16,256]{1,0:T(8,128)(2,1)S(1)}, bf16[16,256]{1,0:T(8,128)(2,1)}, u32[]{:S(2)}) copy-start(bf16[16,256]{1,0:T(8,128)(2,1)} %param.7) | copy-start | bytes 24580
  6.5 63.2 %copy-start.4 = (bf16[16,1,128,256]{3,2,1,0:T(8,128)(2,1)S(1)}, bf16[16,1,128,256]{3,2,1,0:T(8,128)(2,1)}, u32[]{:S(2)}) copy-start(bf16[16,1,128,256]{3,2,1,0:T(8,128)(2,1)} %param.9) | copy-start | bytes 3145732
  65.9 11.8 %all-to-all-start = ((f32[16,16,2]{1,2,0:T(2,128)}), f32[16,16,2]{1,2,0:T(2,128)S(1)}, u32[]{:S(2)}, u32[]{:S(2)}) async-start(f32[16,16,2]{1,2,0:T(2,128)} %copy.53), calls=%async_computation | async-start | bytes 32768 | tf_op jit(solution)/shard_map/all_to_all | solution.py:115
  73.6 2.5 copy-start.1
  77.7 19.0 %all-to-all-start.1 = ((f32[16,16,256]{2,1,0:T(8,128)}), f32[16,16,256]{2,1,0:T(8,128)S(1)}, u32[]{:S(2)}, u32[]{:S(2)}) async-start(f32[16,16,256]{2,1,0:T(8,128)} %reshape.281), calls=%async_computation.1 | async-start | bytes 524288 | tf_op jit(solution)/shard_map/all_to_all | solution.py:114
  85.0 204.8 %reduce-scatter.2.cloned.1.call-start = ((), (), s32[]{:S(2)}) async-start(), calls=%async_computation.3 | async-start | bytes 270336 | tf_op jit(solution)/shard_map/reduce_scatter | solution.py:129
Sparse Core Ops, SparseCore 0:
  98.1 191.6 reduce-scatter.1
where the time goes:
time: 303 us; the launch traced here: 298 us
  waiting for transfers between devices  202 us (67%)
  blocking collectives  50.4 us (17%)
  between operations  14.3 us (5%)
  starting transfers between devices  10.8 us (4%)
  local copies, waits for them, and re-layouts  10.2 us (3%)
  matrix products  5.66 us (2%)
  other arithmetic  4.34 us (1%)
    reduce_scatter x1, waiting for transfers between devices, shards(): lax.psum_scatter(partial_proj, 'tp', scatter_dimension=1, tiled=True)  192 us
    all_gather x1, blocking collectives, shards(): lax.all_gather(borrowed, 'inst', axis=0, tiled=True)  21.2 us
    all_gather x1, blocking collectives, shards(): query_all = lax.all_gather(queries, 'inst', axis=0, tiled=True)  19.4 us
    all_to_all x1, waiting for transfers between devices, shards(): lax.all_to_all(sent_out, 'inst', split_axis=0, concat_axis=0, tiled=True)  10.5 us
    unnamed x1, blocking collectives  9.77 us
    all_to_all x1, starting transfers between devices, shards(): lax.all_to_all(sent_out, 'inst', split_axis=0, concat_axis=0, tiled=True)  7.27 us
  transfers between devices with their start and end apart: 3, of which 2 were waited for; matrix products, arithmetic and copies ran while one was open for 3% of the time, Pallas kernels for 0%

commit v1 on v0

v1 whole, which is shorter than its diff:
```python
import functools
import math

import jax
import jax.numpy as jnp
from jax import lax
from jax.experimental import pallas as pl
from jax.experimental.pallas import tpu as pltpu
from jax.sharding import PartitionSpec as P

HD = 128
PAGE = 128
RANKS = 2
SENTINEL = -1e30
F32 = jnp.float32
BF16 = jnp.bfloat16
I32 = jnp.int32


def column(values, shape):
    row = lax.broadcasted_iota(I32, shape, 0)
    out = jnp.full(shape, values[0], I32)
    for r in range(1, len(values)):
        out = jnp.where(row == r, values[r], out)
    return out


def dot(a, b, dims=((1,), (0,))):
    return lax.dot_general(a, b, (dims, ((), ())), preferred_element_type=F32)


def by_head(x):
    return jnp.concatenate([x[:, :HD], x[:, HD:]], axis=0)


def by_lane(x):
    rows = x.shape[0] // 2
    return jnp.concatenate([x[:rows], x[rows:]], axis=1)


def fused(
    n_inst, nz, nx,
    q_hbm, home_hbm, lent_hbm, table_hbm, borrowed_hbm, lengths_hbm, weight_hbm,
    out_ref,
    q_v, home_v, lent_v, weight_v, table_s, borrowed_s, lengths_s,
    ask_out, ask_in, count_out, count_in, part_out, part_in, stat_out, stat_in, proj_out, proj_in,
    load_sem, send_sem, recv_sem,
):
    n_tp = nz * nx
    slots = lent_v.shape[0]
    reqs = q_v.shape[0]
    me = lax.axis_index("inst")
    tp = lax.axis_index("tp")
    my_z, my_x = tp // nx, tp % nx
    scale = 1.0 / math.sqrt(HD)

    loads = []
    for i, (src, dst) in enumerate(
        [
            (table_hbm, table_s),
            (borrowed_hbm, borrowed_s),
            (lengths_hbm, lengths_s),
            (q_hbm, q_v),
            (home_hbm, home_v),
            (lent_hbm, lent_v),
            (weight_hbm, weight_v),
        ]
    ):
        copy = pltpu.make_async_copy(src, dst, load_sem.at[i])
        copy.start()
        loads.append(copy)

    barrier = pltpu.get_barrier_semaphore()
    for k in range(1, n_inst):
        pl.semaphore_signal(barrier, 1, device_id={"inst": (me + k) % n_inst})
    for k in range(1, n_tp):
        pl.semaphore_signal(barrier, 1, device_id={"tp": (tp + k) % n_tp})

    for copy in loads[:4]:
        copy.wait()

    table = [[table_s[r, j] for j in range(RANKS)] for r in range(reqs)]
    length = [lengths_s[r] for r in range(reqs)]
    beyond = [
        length[r] - PAGE * sum((t >= 0).astype(I32) for t in table[r]) for r in range(reqs)
    ]
    shape = (reqs, 128)
    borrow = [column([borrowed_s[r, j] for r in range(reqs)], shape) for j in range(RANKS)]
    left = column(beyond, shape)
    counted = [jnp.clip(left - PAGE * j, 0, PAGE).astype(F32) for j in range(RANKS)]
    lane = lax.broadcasted_iota(I32, shape, 1)
    total_slots = n_inst * slots
    wanted, counts = [], []
    for base in range(0, total_slots, 128):
        hit = [b == lane + base for b in borrow]
        wanted.append((hit[0] | hit[1]).astype(F32))
        both = jnp.where(hit[0], counted[0], 0.0) + jnp.where(hit[1], counted[1], 0.0)
        counts.append(jnp.sum(both, axis=0, keepdims=True))
    wanted = jnp.concatenate(wanted, axis=1)[:, :total_slots].astype(BF16)
    counts = jnp.concatenate(counts, axis=1)
    q = q_v[...]
    asked = dot(wanted, q, ((0,), (0,))).astype(BF16)
    ask_out[...] = asked.reshape(n_inst, slots, 2 * HD)
    count_out[...] = counts
    ask_in[n_inst - 1] = ask_out[me]
    count_in[n_inst - 1] = counts

    pl.semaphore_wait(barrier, n_inst + n_tp - 2)

    def send(src, dst, phase, to):
        pltpu.make_async_remote_copy(
            src_ref=src, dst_ref=dst, send_sem=send_sem.at[phase], recv_sem=recv_sem.at[phase], device_id=to
        ).start()

    def arrive(ref, count, phase):
        part = ref.at[pl.ds(0, count)]
        pltpu.make_async_copy(part, part, recv_sem.at[phase]).wait()

    def sent(ref, count, phase):
        part = ref.at[pl.ds(0, count)]
        pltpu.make_async_copy(part, part, send_sem.at[phase]).wait()

    order = sorted(range(1, n_inst), key=lambda k: -min(k, n_inst - k))
    for k in order:
        to = (me + k) % n_inst
        send(ask_out.at[to], ask_in.at[k - 1], 0, {"inst": to})
        send(count_out, count_in.at[k - 1], 1, {"inst": to})

    row = lax.broadcasted_iota(I32, (2 * reqs, PAGE), 0) % reqs
    token = lax.broadcasted_iota(I32, (2 * reqs, PAGE), 1)
    q2 = by_head(q)
    loads[4].wait()
    scores = [jnp.zeros((2 * reqs, PAGE), F32) for _ in range(RANKS)]
    usable = [jnp.zeros((2 * reqs, PAGE), I32) for _ in range(RANKS)]
    for r in range(reqs):
        for j in range(RANKS):
            page = jnp.maximum(table[r][j], 0)
            s = dot(q2, home_v[page, 0, :, :HD], ((1,), (1,)))
            scores[j] = jnp.where(row == r, s, scores[j])
            here = jnp.where(table[r][j] >= 0, length[r] - PAGE * j, 0)
            usable[j] = jnp.where(row == r, here, usable[j])
    usable = [token < u for u in usable]
    scores = [jnp.where(u, s * scale, SENTINEL) for u, s in zip(usable, scores)]
    home_max = jnp.max(jnp.maximum(scores[0], scores[1]), axis=1, keepdims=True)
    home_w = [
        jnp.where(u, jnp.exp(s - home_max), 0.0).astype(BF16) for u, s in zip(usable, scores)
    ]
    home_total = sum(jnp.sum(w.astype(F32), axis=1, keepdims=True) for w in home_w)
    home_sum = jnp.zeros((2 * reqs, HD), F32)
    for r in range(reqs):
        o = 0.0
        for j in range(RANKS):
            page = jnp.maximum(table[r][j], 0)
            o = o + dot(home_w[j], home_v[page, 0, :, HD:])
        home_sum = jnp.where(row == r, o, home_sum)

    loads[5].wait()
    arrive(ask_in, n_inst - 1, 0)
    arrive(count_in, n_inst - 1, 1)
    q_lent = ask_in[0]
    for k in range(1, n_inst):
        q_lent = q_lent + ask_in[k]
    q_lent = by_head(q_lent)
    count_row = jnp.sum(count_in[...], axis=0)
    wide = (slots, count_row.shape[1])
    mine = lax.broadcasted_iota(I32, wide, 1) == me * slots + lax.broadcasted_iota(I32, wide, 0)
    count_col = jnp.sum(jnp.where(mine, count_row, 0.0), axis=1, keepdims=True)
    count_col = jnp.concatenate([count_col, count_col], axis=0)
    lrow = lax.broadcasted_iota(I32, (2 * slots, PAGE), 0)
    lslot = lrow % slots
    llane = lax.broadcasted_iota(I32, (2 * slots, PAGE), 1)
    s = jnp.zeros((2 * slots, PAGE), F32)
    for p in range(slots):
        s = jnp.where(lslot == p, dot(q_lent, lent_v[p, 0, :, :HD], ((1,), (1,))), s)
    ok = llane < count_col.astype(I32)
    s = jnp.where(ok, s * scale, SENTINEL)
    lent_max = jnp.max(s, axis=1, keepdims=True)
    w = jnp.where(ok, jnp.exp(s - lent_max), 0.0).astype(BF16)
    lent_total = jnp.sum(w.astype(F32), axis=1, keepdims=True)
    o = jnp.zeros((2 * slots, HD), F32)
    for p in range(slots):
        o = jnp.where(lslot == p, dot(w, lent_v[p, 0, :, HD:]), o)
    part = by_lane(o).astype(BF16)
    stats = jnp.where(llane == lrow, lent_max, 0.0) + jnp.where(
        llane == lrow + 2 * slots, lent_total, 0.0
    )
    stats = jnp.sum(stats, axis=0, keepdims=True)
    part_out[...] = part
    stat_out[...] = stats
    part_in[n_inst - 1] = part
    stat_in[n_inst - 1] = stats
    for k in order:
        to = (me + k) % n_inst
        send(stat_out, stat_in.at[k - 1], 3, {"inst": to})
        send(part_out, part_in.at[k - 1], 2, {"inst": to})

    two = jnp.concatenate(borrow, axis=0)
    gather = []
    for base in range(0, total_slots, 128):
        i = base + lax.broadcasted_iota(I32, two.shape, 1)
        name = (me - i // slots - 1) % n_inst * slots + i % slots
        gather.append((two == name).astype(F32))
    gather = jnp.concatenate(gather, axis=1)[:, :total_slots].astype(BF16)
    lane2 = lax.broadcasted_iota(I32, two.shape, 1)
    lender = ((me - lane2 - 1) % n_inst == two // slots) & (lane2 < n_inst) & (two >= 0)
    lender = lender[:, :n_inst].astype(F32).astype(BF16)
    slot = jnp.where(two >= 0, two % slots, -1)

    arrive(stat_in, n_inst - 1, 3)
    left_over = stat_in[...].reshape(n_inst, 128)
    found = jnp.zeros(two.shape, F32)
    for _ in range(3):
        piece = left_over.astype(BF16)
        found = found + dot(lender, piece)
        left_over = left_over - piece.astype(F32)
    present = two[:, :1] >= 0

    def pick(kind, absent):
        value = jnp.sum(jnp.where(lane2 == slot + kind * slots, found, 0.0), axis=1, keepdims=True)
        value = jnp.where((slot[:, :1] >= 0), value, absent)
        return [value[j * reqs : (j + 1) * reqs] for j in range(RANKS)]

    max0, max1 = pick(0, SENTINEL), pick(1, SENTINEL)
    tot0, tot1 = pick(2, 0.0), pick(3, 0.0)
    page_max = [jnp.concatenate([max0[j], max1[j]], axis=0) for j in range(RANKS)]
    page_total = [jnp.concatenate([tot0[j], tot1[j]], axis=0) for j in range(RANKS)]
    summit = jnp.maximum(home_max, jnp.maximum(page_max[0], page_max[1]))
    home_share = jnp.exp(home_max - summit)
    share = [jnp.exp(m - summit) for m in page_max]
    total = home_share * home_total + share[0] * page_total[0] + share[1] * page_total[1]
    total = jnp.maximum(total, 1.0)
    arrive(part_in, n_inst - 1, 2)
    got = dot(gather, part_in[...].reshape(total_slots, 2 * HD))
    attended = home_share * home_sum
    for j in range(RANKS):
        attended = attended + share[j] * by_head(got[j * reqs : (j + 1) * reqs])
    attended = by_lane(attended / total).astype(BF16)

    loads[6].wait()
    steps = sorted(range(nz), key=lambda d: -min(d, nz - d))
    for n, dz in enumerate(steps):
        z = (my_z + dz) % nz
        start = pl.multiple_of(z * (nx * 128), nx * 128)
        block = dot(attended, weight_v[:, pl.ds(start, nx * 128)]).astype(BF16)
        for x in range(nx):
            proj_out[n * nx + x] = block[:, x * 128 : (x + 1) * 128]
        for x in range(nx):
            place = n * nx + (x - my_x) % nx
            to = {"tp": z * nx + x}
            if dz == 0:

                @pl.when(x != my_x)
                def _():
                    send(proj_out.at[n * nx + x], proj_in.at[place - 1], 4, to)
            else:
                send(proj_out.at[n * nx + x], proj_in.at[place], 4, to)
    result = proj_out[(nz - 1) * nx + my_x].astype(F32)
    arrive(proj_in, n_tp - 1, 4)
    result = result + jnp.sum(proj_in[...].astype(F32), axis=0)
    out_ref[...] = result.astype(out_ref.dtype)

    sent(ask_in, n_inst - 1, 0)
    sent(count_in, n_inst - 1, 1)
    sent(part_in, n_inst - 1, 2)
    sent(stat_in, n_inst - 1, 3)
    sent(proj_in, n_tp - 1, 4)


def shards(nx, queries, home_kv, lent_kv, page_table, borrowed, lengths, out_weight):
    n_inst, n_tp = lax.axis_size("inst"), lax.axis_size("tp")
    reqs = queries.shape[0]
    slots = lent_kv.shape[0]
    cols = out_weight.shape[1] // n_tp
    lanes = -(-n_inst * slots // 128) * 128
    return pl.pallas_call(
        functools.partial(fused, n_inst, n_tp // nx, nx),
        out_shape=jax.ShapeDtypeStruct((reqs, cols), BF16),
        in_specs=[pl.BlockSpec(memory_space=pl.ANY)] * 7,
        out_specs=pl.BlockSpec(memory_space=pltpu.VMEM),
        scratch_shapes=[
            pltpu.VMEM(queries.shape, BF16),
            pltpu.VMEM(home_kv.shape, BF16),
            pltpu.VMEM(lent_kv.shape, BF16),
            pltpu.VMEM(out_weight.shape, BF16),
            pltpu.SMEM(page_table.shape, I32),
            pltpu.SMEM(borrowed.shape, I32),
            pltpu.SMEM(lengths.shape, I32),
            pltpu.VMEM((n_inst, slots, 2 * HD), BF16),
            pltpu.VMEM((n_inst, slots, 2 * HD), BF16),
            pltpu.VMEM((1, lanes), F32),
            pltpu.VMEM((n_inst, 1, lanes), F32),
            pltpu.VMEM((slots, 2 * HD), BF16),
            pltpu.VMEM((n_inst, slots, 2 * HD), BF16),
            pltpu.VMEM((1, 128), F32),
            pltpu.VMEM((n_inst, 1, 128), F32),
            pltpu.VMEM((n_tp, reqs, cols), BF16),
            pltpu.VMEM((n_tp - 1, reqs, cols), BF16),
            pltpu.SemaphoreType.DMA((7,)),
            pltpu.SemaphoreType.DMA((5,)),
            pltpu.SemaphoreType.DMA((5,)),
        ],
        compiler_params=pltpu.CompilerParams(
            collective_id=0, has_side_effects=True, vmem_limit_bytes=40 * 1024 * 1024
        ),
    )(queries, home_kv, lent_kv, page_table, borrowed, lengths, out_weight)


def solution(mesh):
    n_tp = mesh.shape["tp"]
    nx = 4 if n_tp % 4 == 0 else 1
    placed = (
        P("inst", "tp"),
        P("inst", "tp", None, None),
        P("inst", "tp", None, None),
        P("inst", None),
        P("inst", None),
        P("inst"),
        P("tp", None),
    )
    return jax.shard_map(
        functools.partial(shards, nx), mesh=mesh, in_specs=placed, out_specs=P("inst", "tp"), check_vma=False
    )
```

time: 303 us -> 42.3 us (0.14); the launches traced: 298 us -> 42 us
  waiting for transfers between devices: 202 us -> 0 us
  blocking collectives: 50.4 us -> 0 us
  Pallas kernels: 0 us -> 34.3 us
  between operations: 14.3 us -> 0.02 us
  starting transfers between devices: 10.8 us -> 0 us
  matrix products: 5.66 us -> 0 us
  other arithmetic: 4.34 us -> 0 us
    reduce_scatter x1 -> x0, waiting for transfers between devices: 192 us -> none  [shards(): lax.psum_scatter(partial_proj, 'tp', scatter_dimension=1, tiled=True)]
    all_gather x2 -> x0, blocking collectives: 40.6 us -> none  [the longest x1 21.2 us: shards(): lax.all_gather(borrowed, 'inst', axis=0, tiled=True)]
    pallas_call x0 -> x1, Pallas kernels: none -> 34.3 us  [shards(): pl.pallas_call(functools.partial(fused, n_inst, n_tp // nx, nx), out_shap...]
    all_to_all x2 -> x0, starting transfers between devices: 10.7 us -> none  [the longest x1 7.27 us: shards(): lax.all_to_all(sent_out, 'inst', split_axis=0, concat_axis=0, tiled=True)]
    all_to_all x2 -> x0, waiting for transfers between devices: 10.5 us -> none  [the longest x1 10.5 us: shards(): lax.all_to_all(sent_out, 'inst', split_axis=0, concat_axis=0, tiled=True)]
    unnamed x1 -> x0, blocking collectives: 9.77 us -> none
    unnamed x12 -> x13, local copies, waits for them, and re-layouts: 1.29 us -> 7.68 us
    dot_general x7 -> x0, matrix products: 5.66 us -> none  [the longest x1 1.85 us: shards(): jnp.einsum('rgd,rptd->rpgt', query_heads, home_pages[..., :HD], preferred...]
  transfers between devices with their start and end apart: 3 -> 0, of which waited for: 2 -> 0; matrix products, arithmetic and copies ran while one was open for 3% -> 0% of each run, Pallas kernels for 0% -> 0%
where the time goes in v1:
time: 42.3 us; the launch traced here: 42 us
  Pallas kernels  34.3 us (81%)
  local copies, waits for them, and re-layouts  7.68 us (18%)
    pallas_call x1, Pallas kernels, shards(): pl.pallas_call(functools.partial(fused, n_inst, n_tp // nx, nx), out_shap...  34.3 us
    unnamed x13, local copies, waits for them, and re-layouts  7.68 us

profile of v1, /device:TPU:1, one launch (start us, length us, event | category | flops | bytes accessed | tf_op | source)
XLA Modules:
  0.0 42.0 jit_solution(971365209499457916)
XLA Ops:
  0.0 0.8 %copy.8.table_hbm = s32[16,2]{1,0:T(8,128)S(1)} copy(s32[16,2]{0,1:T(2,128)} %param.10) | data formatting | bytes 256 | tf_op args[3]
  0.8 0.8 %copy.9.borrowed_hbm = s32[16,2]{1,0:T(8,128)S(1)} copy(s32[16,2]{0,1:T(2,128)} %param.11) | data formatting | bytes 256 | tf_op args[4]
  1.5 0.0 copy-start
  1.5 1.6 %copy-done = bf16[256,4096]{1,0:T(8,128)(2,1)S(1)} copy-done((bf16[256,4096]{1,0:T(8,128)(2,1)S(1)}, bf16[256,4096]{1,0:T(8,128)(2,1)}, u32[]{:S(2)}) %copy-start) | copy-done | bytes 2097176
  3.1 0.0 copy-start.1
  3.1 1.4 %copy-done.1 = bf16[24,1,128,256]{3,2,1,0:T(8,128)(2,1)S(1)} copy-done((bf16[24,1,128,256]{3,2,1,0:T(8,128)(2,1)S(1)}, bf16[24,1,128,256]{3,2,1,0:T(8,128)(2,1)}, u32[]{:S(2)}) %copy-start.1) | copy-done | bytes 1572888
  4.5 0.0 copy-start.2
  4.5 1.2 %copy-done.2 = bf16[16,1,128,256]{3,2,1,0:T(8,128)(2,1)S(1)} copy-done((bf16[16,1,128,256]{3,2,1,0:T(8,128)(2,1)S(1)}, bf16[16,1,128,256]{3,2,1,0:T(8,128)(2,1)}, u32[]{:S(2)}) %copy-start.2) | copy-done | bytes 1048600
  5.7 0.0 copy-start.3
  5.7 0.7 %copy-done.3 = bf16[16,256]{1,0:T(8,128)(2,1)S(1)} copy-done((bf16[16,256]{1,0:T(8,128)(2,1)S(1)}, bf16[16,256]{1,0:T(8,128)(2,1)}, u32[]{:S(2)}) %copy-start.3) | copy-done | bytes 8216
  6.4 0.0 copy-start.4
  6.4 0.7 %copy-done.4 = s32[16]{0:T(128)S(1)} copy-done((s32[16]{0:T(128)S(1)}, s32[16]{0:T(128)}, u32[]{:S(2)}) %copy-start.4) | copy-done | bytes 88
  7.1 34.3 %shard_map.73 = bf16[16,128]{1,0:T(8,128)(2,1)S(1)} custom-call(bf16[16,256]{1,0:T(8,128)(2,1)S(1)} %copy-done.3, bf16[24,1,128,256]{3,2,1,0:T(8,128)(2,1)S(1)} %copy-done.1, bf16[16,1,128,256]{3,2,1,0:T(8,128)(2,1)S(1)} %copy-done.2, s32[16,2]{1,0:T(8,128)S(1)} %copy.8.table_hbm, s32[16,2]{1,0:T(8,128)S(1)} %copy.9.borrowed_hbm, s32[16]{0:T(128)S(1)} %copy-done.4, ...), custom_call_target="tpu_custom_call" | custom-call | tf_op jit(solution)/shard_map/pallas_call | solution.py:275
  41.4 0.6 %copy.11 = bf16[16,128]{1,0:T(8,128)(2,1)} copy(bf16[16,128]{1,0:T(8,128)(2,1)S(1)} %shard_map.73) | data formatting | bytes 8192
Async XLA Ops:
  1.5 1.6 %copy-start = (bf16[256,4096]{1,0:T(8,128)(2,1)S(1)}, bf16[256,4096]{1,0:T(8,128)(2,1)}, u32[]{:S(2)}) copy-start(bf16[256,4096]{1,0:T(8,128)(2,1)} %weight_hbm.1) | copy-start | bytes 6291460
  3.1 1.4 %copy-start.1 = (bf16[24,1,128,256]{3,2,1,0:T(8,128)(2,1)S(1)}, bf16[24,1,128,256]{3,2,1,0:T(8,128)(2,1)}, u32[]{:S(2)}) copy-start(bf16[24,1,128,256]{3,2,1,0:T(8,128)(2,1)} %home_hbm.1) | copy-start | bytes 4718596
  4.5 1.2 %copy-start.2 = (bf16[16,1,128,256]{3,2,1,0:T(8,128)(2,1)S(1)}, bf16[16,1,128,256]{3,2,1,0:T(8,128)(2,1)}, u32[]{:S(2)}) copy-start(bf16[16,1,128,256]{3,2,1,0:T(8,128)(2,1)} %lent_hbm.1) | copy-start | bytes 3145732
  5.7 0.7 %copy-start.3 = (bf16[16,256]{1,0:T(8,128)(2,1)S(1)}, bf16[16,256]{1,0:T(8,128)(2,1)}, u32[]{:S(2)}) copy-start(bf16[16,256]{1,0:T(8,128)(2,1)} %q_hbm.1) | copy-start | bytes 24580
  6.4 0.7 %copy-start.4 = (s32[16]{0:T(128)S(1)}, s32[16]{0:T(128)}, u32[]{:S(2)}) copy-start(s32[16]{0:T(128)} %lengths_hbm.1) | copy-start | bytes 196

commit v2 on v1

--- a/solution.py
+++ b/solution.py
@@ -44,7 +44,7 @@
     out_ref,
     q_v, home_v, lent_v, weight_v, table_s, borrowed_s, lengths_s,
     ask_out, ask_in, count_out, count_in, part_out, part_in, stat_out, stat_in, proj_out, proj_in,
-    load_sem, send_sem, recv_sem,
+    load_sem, send_sem, recv_sem, here_sem,
 ):
     n_tp = nz * nx
     slots = lent_v.shape[0]
@@ -53,6 +53,33 @@
     tp = lax.axis_index("tp")
     my_z, my_x = tp // nx, tp % nx
     scale = 1.0 / math.sqrt(HD)
+
+    barrier = pltpu.get_barrier_semaphore()
+    order = sorted(range(1, n_inst), key=lambda k: -min(k, n_inst - k))
+    rounds = []
+    step = 1
+    while step <= nz // 2:
+        rounds.append(sorted({step, nz - step}))
+        step *= 2
+
+    def along_z(d):
+        return {"tp": (my_z + d) % nz * nx + my_x}
+
+    for k in order:
+        pl.semaphore_signal(barrier, 1, device_id={"inst": (me + k) % n_inst})
+    for d in range(1, nx):
+        pl.semaphore_signal(barrier, 1, device_id={"tp": my_z * nx + (my_x + d) % nx})
+    for d in rounds[0] if rounds else []:
+        pl.semaphore_signal(barrier, 1, device_id=along_z(d))
+    greeted = n_inst - 1 + nx - 1 + (len(rounds[0]) if rounds else 0)
+
+    def tell(i):
+        for d in rounds[i] if i < len(rounds) else []:
+            pl.semaphore_signal(here_sem.at[i], 1, device_id=along_z(d))
+
+    def told(i):
+        if i < len(rounds):
+            pl.semaphore_wait(here_sem.at[i], len(rounds[i]))
 
     loads = []
     for i, (src, dst) in enumerate(
@@ -70,22 +97,16 @@
         copy.start()
         loads.append(copy)
 
-    barrier = pltpu.get_barrier_semaphore()
-    for k in range(1, n_inst):
-        pl.semaphore_signal(barrier, 1, device_id={"inst": (me + k) % n_inst})
-    for k in range(1, n_tp):
-        pl.semaphore_signal(barrier, 1, device_id={"tp": (tp + k) % n_tp})
-
     for copy in loads[:4]:
         copy.wait()
 
-    table = [[table_s[r, j] for j in range(RANKS)] for r in range(reqs)]
+    table = [[table_s[j, r] for j in range(RANKS)] for r in range(reqs)]
     length = [lengths_s[r] for r in range(reqs)]
     beyond = [
         length[r] - PAGE * sum((t >= 0).astype(I32) for t in table[r]) for r in range(reqs)
     ]
     shape = (reqs, 128)
-    borrow = [column([borrowed_s[r, j] for r in range(reqs)], shape) for j in range(RANKS)]
+    borrow = [column([borrowed_s[j, r] for r in range(reqs)], shape) for j in range(RANKS)]
     left = column(beyond, shape)
     counted = [jnp.clip(left - PAGE * j, 0, PAGE).astype(F32) for j in range(RANKS)]
     lane = lax.broadcasted_iota(I32, shape, 1)
@@ -105,13 +126,25 @@
     ask_in[n_inst - 1] = ask_out[me]
     count_in[n_inst - 1] = counts
 
-    pl.semaphore_wait(barrier, n_inst + n_tp - 2)
+    pl.semaphore_wait(barrier, greeted)
 
     def send(src, dst, phase, to):
         pltpu.make_async_remote_copy(
             src_ref=src, dst_ref=dst, send_sem=send_sem.at[phase], recv_sem=recv_sem.at[phase], device_id=to
         ).start()
 
+    n_chip = n_inst // 2
+
+    def to_chips(chips, act):
+        for y in chips:
+
+            @pl.when(y != me // 2)
+            def _():
+                act(2 * y + 1)
+                act(2 * y)
+
+        act(me + 1 - 2 * (me % 2))
+
     def arrive(ref, count, phase):
         part = ref.at[pl.ds(0, count)]
         pltpu.make_async_copy(part, part, recv_sem.at[phase]).wait()
@@ -120,11 +153,14 @@
         part = ref.at[pl.ds(0, count)]
         pltpu.make_async_copy(part, part, send_sem.at[phase]).wait()
 
-    order = sorted(range(1, n_inst), key=lambda k: -min(k, n_inst - k))
-    for k in order:
-        to = (me + k) % n_inst
-        send(ask_out.at[to], ask_in.at[k - 1], 0, {"inst": to})
-        send(count_out, count_in.at[k - 1], 1, {"inst": to})
+    def ask(to):
+        place = (to - me - 1) % n_inst
+        send(ask_out.at[to], ask_in.at[place], 0, {"inst": to})
+        send(count_out, count_in.at[place], 1, {"inst": to})
+
+    to_chips(sorted(range(n_chip), key=lambda y: abs(y - n_chip // 2)), ask)
+
+    tell(0)
 
     row = lax.broadcasted_iota(I32, (2 * reqs, PAGE), 0) % reqs
     token = lax.broadcasted_iota(I32, (2 * reqs, PAGE), 1)
@@ -153,6 +189,9 @@
             page = jnp.maximum(table[r][j], 0)
             o = o + dot(home_w[j], home_v[page, 0, :, HD:])
         home_sum = jnp.where(row == r, o, home_sum)
+
+    told(0)
+    tell(1)
 
     loads[5].wait()
     arrive(ask_in, n_inst - 1, 0)
@@ -189,10 +228,15 @@
     stat_out[...] = stats
     part_in[n_inst - 1] = part
     stat_in[n_inst - 1] = stats
-    for k in order:
-        to = (me + k) % n_inst
-        send(stat_out, stat_in.at[k - 1], 3, {"inst": to})
-        send(part_out, part_in.at[k - 1], 2, {"inst": to})
+    def answer(to):
+        place = (to - me - 1) % n_inst
+        send(stat_out, stat_in.at[place], 3, {"inst": to})
+        send(part_out, part_in.at[place], 2, {"inst": to})
+
+    to_chips(sorted(range(n_chip), key=lambda y: min(y, n_chip - y)), answer)
+
+    told(1)
+    tell(2)
 
     two = jnp.concatenate(borrow, axis=0)
     gather = []
@@ -237,24 +281,28 @@
     attended = by_lane(attended / total).astype(BF16)
 
     loads[6].wait()
-    steps = sorted(range(nz), key=lambda d: -min(d, nz - d))
-    for n, dz in enumerate(steps):
-        z = (my_z + dz) % nz
+    told(2)
+    def project(z):
         start = pl.multiple_of(z * (nx * 128), nx * 128)
         block = dot(attended, weight_v[:, pl.ds(start, nx * 128)]).astype(BF16)
         for x in range(nx):
-            proj_out[n * nx + x] = block[:, x * 128 : (x + 1) * 128]
-        for x in range(nx):
-            place = n * nx + (x - my_x) % nx
-            to = {"tp": z * nx + x}
-            if dz == 0:
-
-                @pl.when(x != my_x)
-                def _():
-                    send(proj_out.at[n * nx + x], proj_in.at[place - 1], 4, to)
-            else:
-                send(proj_out.at[n * nx + x], proj_in.at[place], 4, to)
-    result = proj_out[(nz - 1) * nx + my_x].astype(F32)
+            proj_out[z * nx + x] = block[:, x * 128 : (x + 1) * 128]
+
+    def hand_over(z, x):
+        place = (z - my_z) % nz * nx + (x - my_x) % nx - 1
+        send(proj_out.at[z * nx + x], proj_in.at[place], 4, {"tp": z * nx + x})
+
+    for z in range(nz):
+        project(z)
+
+        @pl.when(z != my_z)
+        def _():
+            for x in range(nx):
+                hand_over(z, x)
+
+    for d in range(1, nx):
+        hand_over(my_z, (my_x + d) % nx)
+    result = proj_out[tp].astype(F32)
     arrive(proj_in, n_tp - 1, 4)
     result = result + jnp.sum(proj_in[...].astype(F32), axis=0)
     out_ref[...] = result.astype(out_ref.dtype)
@@ -275,15 +323,15 @@
     return pl.pallas_call(
         functools.partial(fused, n_inst, n_tp // nx, nx),
         out_shape=jax.ShapeDtypeStruct((reqs, cols), BF16),
-        in_specs=[pl.BlockSpec(memory_space=pl.ANY)] * 7,
+        in_specs=[pl.BlockSpec(memory_space=pltpu.HBM)] * 7,
         out_specs=pl.BlockSpec(memory_space=pltpu.VMEM),
         scratch_shapes=[
             pltpu.VMEM(queries.shape, BF16),
             pltpu.VMEM(home_kv.shape, BF16),
             pltpu.VMEM(lent_kv.shape, BF16),
             pltpu.VMEM(out_weight.shape, BF16),
-            pltpu.SMEM(page_table.shape, I32),
-            pltpu.SMEM(borrowed.shape, I32),
+            pltpu.SMEM(page_table.shape[::-1], I32),
+            pltpu.SMEM(borrowed.shape[::-1], I32),
             pltpu.SMEM(lengths.shape, I32),
             pltpu.VMEM((n_inst, slots, 2 * HD), BF16),
             pltpu.VMEM((n_inst, slots, 2 * HD), BF16),
@@ -298,11 +346,12 @@
             pltpu.SemaphoreType.DMA((7,)),
             pltpu.SemaphoreType.DMA((5,)),
             pltpu.SemaphoreType.DMA((5,)),
+            pltpu.SemaphoreType.REGULAR((3,)),
         ],
         compiler_params=pltpu.CompilerParams(
             collective_id=0, has_side_effects=True, vmem_limit_bytes=40 * 1024 * 1024
         ),
-    )(queries, home_kv, lent_kv, page_table, borrowed, lengths, out_weight)
+    )(*[pltpu.with_memory_space_constraint(x, pltpu.HBM) for x in (queries, home_kv, lent_kv, page_table.T, borrowed.T, lengths, out_weight)])
 
 
 def solution(mesh):

time: 42.3 us -> 33.4 us (0.79)
  the two profiles are of different devices: /device:TPU:1 before, /device:TPU:16 now
where the time goes in v2:
time: 33.4 us; the launch traced here: 33.3 us
  Pallas kernels  32.7 us (98%)
  local copies, waits for them, and re-layouts  0.6 us (2%)
    pallas_call x1, Pallas kernels, shards(): pl.pallas_call(functools.partial(fused, n_inst, n_tp // nx, nx), out_shap...  32.7 us

profile of v2, /device:TPU:16, one launch (start us, length us, event | category | flops | bytes accessed | tf_op | source)
XLA Modules:
  0.0 33.3 jit_solution(17503038383405795232)
XLA Ops:
  0.0 32.7 %shard_map.73 = bf16[16,128]{1,0:T(8,128)(2,1)S(1)} custom-call(bf16[16,256]{1,0:T(8,128)(2,1)} %q_hbm.1, bf16[24,1,128,256]{3,2,1,0:T(8,128)(2,1)} %home_hbm.1, bf16[16,1,128,256]{3,2,1,0:T(8,128)(2,1)} %lent_hbm.1, s32[2,16]{1,0:T(2,128)} %bitcast.2, s32[2,16]{1,0:T(2,128)} %bitcast.3, s32[16]{0:T(128)} %lengths_hbm.1, bf16[256,4096]{1,0:T(8,128)(2,1)} %weight_hbm.1), custom_call_target="tpu_custom_call" | custom-call | tf_op jit(solution)/shard_map/pallas_call | solution.py:323
  32.7 0.6 %copy.9 = bf16[16,128]{1,0:T(8,128)(2,1)} copy(bf16[16,128]{1,0:T(8,128)(2,1)S(1)} %shard_map.73) | data formatting | bytes 8192

commit v3 on v2

--- a/solution.py
+++ b/solution.py
@@ -44,7 +44,7 @@
     out_ref,
     q_v, home_v, lent_v, weight_v, table_s, borrowed_s, lengths_s,
     ask_out, ask_in, count_out, count_in, part_out, part_in, stat_out, stat_in, proj_out, proj_in,
-    load_sem, send_sem, recv_sem, here_sem,
+    keys_v, load_sem, send_sem, recv_sem, here_sem,
 ):
     n_tp = nz * nx
     slots = lent_v.shape[0]
@@ -140,8 +140,8 @@
 
             @pl.when(y != me // 2)
             def _():
-                act(2 * y + 1)
-                act(2 * y)
+                act(2 * y + 1 - me % 2)
+                act(2 * y + me % 2)
 
         act(me + 1 - 2 * (me % 2))
 
@@ -194,6 +194,15 @@
     tell(1)
 
     loads[5].wait()
+    for p in range(slots):
+        keys_v[p * HD : (p + 1) * HD] = lent_v[p, 0, :, :HD].T
+    lrow = lax.broadcasted_iota(I32, (2 * slots, PAGE), 0)
+    llane = lax.broadcasted_iota(I32, (2 * slots, PAGE), 1)
+    own = [(lrow % slots == p).astype(F32).astype(BF16) for p in range(slots)]
+
+    def spread(x):
+        return jnp.concatenate([x * o for o in own], axis=1)
+
     arrive(ask_in, n_inst - 1, 0)
     arrive(count_in, n_inst - 1, 1)
     q_lent = ask_in[0]
@@ -205,20 +214,13 @@
     mine = lax.broadcasted_iota(I32, wide, 1) == me * slots + lax.broadcasted_iota(I32, wide, 0)
     count_col = jnp.sum(jnp.where(mine, count_row, 0.0), axis=1, keepdims=True)
     count_col = jnp.concatenate([count_col, count_col], axis=0)
-    lrow = lax.broadcasted_iota(I32, (2 * slots, PAGE), 0)
-    lslot = lrow % slots
-    llane = lax.broadcasted_iota(I32, (2 * slots, PAGE), 1)
-    s = jnp.zeros((2 * slots, PAGE), F32)
-    for p in range(slots):
-        s = jnp.where(lslot == p, dot(q_lent, lent_v[p, 0, :, :HD], ((1,), (1,))), s)
+    s = dot(spread(q_lent), keys_v[...])
     ok = llane < count_col.astype(I32)
     s = jnp.where(ok, s * scale, SENTINEL)
     lent_max = jnp.max(s, axis=1, keepdims=True)
     w = jnp.where(ok, jnp.exp(s - lent_max), 0.0).astype(BF16)
     lent_total = jnp.sum(w.astype(F32), axis=1, keepdims=True)
-    o = jnp.zeros((2 * slots, HD), F32)
-    for p in range(slots):
-        o = jnp.where(lslot == p, dot(w, lent_v[p, 0, :, HD:]), o)
+    o = dot(spread(w), lent_v[:, 0, :, HD:].reshape(slots * PAGE, HD))
     part = by_lane(o).astype(BF16)
     stats = jnp.where(llane == lrow, lent_max, 0.0) + jnp.where(
         llane == lrow + 2 * slots, lent_total, 0.0
@@ -233,7 +235,7 @@
         send(stat_out, stat_in.at[place], 3, {"inst": to})
         send(part_out, part_in.at[place], 2, {"inst": to})
 
-    to_chips(sorted(range(n_chip), key=lambda y: min(y, n_chip - y)), answer)
+    to_chips(sorted(range(n_chip), key=lambda y: min(y, n_chip + 1 - y)), answer)
 
     told(1)
     tell(2)
@@ -343,6 +345,7 @@
             pltpu.VMEM((n_inst, 1, 128), F32),
             pltpu.VMEM((n_tp, reqs, cols), BF16),
             pltpu.VMEM((n_tp - 1, reqs, cols), BF16),
+            pltpu.VMEM((slots * HD, PAGE), BF16),
             pltpu.SemaphoreType.DMA((7,)),
             pltpu.SemaphoreType.DMA((5,)),
             pltpu.SemaphoreType.DMA((5,)),

time: 33.4 us -> 32.9 us (0.985)
  the two profiles are of different devices: /device:TPU:16 before, /device:TPU:1 now
where the time goes in v3:
time: 32.9 us; the launch traced here: 32.4 us
  Pallas kernels  31.8 us (97%)
  local copies, waits for them, and re-layouts  0.6 us (2%)
    pallas_call x1, Pallas kernels, shards(): pl.pallas_call(functools.partial(fused, n_inst, n_tp // nx, nx), out_shap...  31.8 us

profile of v3, /device:TPU:1, one launch (start us, length us, event | category | flops | bytes accessed | tf_op | source)
XLA Modules:
  0.0 32.4 jit_solution(14834933462643037816)
XLA Ops:
  0.0 31.8 %shard_map.73 = bf16[16,128]{1,0:T(8,128)(2,1)S(1)} custom-call(bf16[16,256]{1,0:T(8,128)(2,1)} %q_hbm.1, bf16[24,1,128,256]{3,2,1,0:T(8,128)(2,1)} %home_hbm.1, bf16[16,1,128,256]{3,2,1,0:T(8,128)(2,1)} %lent_hbm.1, s32[2,16]{1,0:T(2,128)} %bitcast.2, s32[2,16]{1,0:T(2,128)} %bitcast.3, s32[16]{0:T(128)} %lengths_hbm.1, bf16[256,4096]{1,0:T(8,128)(2,1)} %weight_hbm.1), custom_call_target="tpu_custom_call" | custom-call | tf_op jit(solution)/shard_map/pallas_call | solution.py:325
  31.8 0.6 %copy.9 = bf16[16,128]{1,0:T(8,128)(2,1)} copy(bf16[16,128]{1,0:T(8,128)(2,1)S(1)} %shard_map.73) | data formatting | bytes 8192

commit v4 on v3

--- a/solution.py
+++ b/solution.py
@@ -43,7 +43,7 @@
     q_hbm, home_hbm, lent_hbm, table_hbm, borrowed_hbm, lengths_hbm, weight_hbm,
     out_ref,
     q_v, home_v, lent_v, weight_v, table_s, borrowed_s, lengths_s,
-    ask_out, ask_in, count_out, count_in, part_out, part_in, stat_out, stat_in, proj_out, proj_in,
+    ask_out, ask_in, ask_relay, count_out, count_in, count_relay, count_sum, part_out, part_in, stat_out, stat_in, proj_out, proj_in,
     keys_v, load_sem, send_sem, recv_sem, here_sem,
 ):
     n_tp = nz * nx
@@ -52,6 +52,16 @@
     me = lax.axis_index("inst")
     tp = lax.axis_index("tp")
     my_z, my_x = tp // nx, tp % nx
+    my_y, my_c = me // 2, me % 2
+    n_chip = n_inst // 2
+    half = n_chip // 2
+    near = [d for d in range(1, n_chip) if d != half]
+    n_near = len(near)
+    far_first = sorted(range(n_near), key=lambda p: -min(near[p], n_chip - near[p]))
+    sibling = me + 1 - 2 * my_c
+
+    def chip_at(dy, other=0):
+        return (my_y + dy) % n_chip * 2 + (my_c + other - 2 * my_c * other)
     scale = 1.0 / math.sqrt(HD)
 
     barrier = pltpu.get_barrier_semaphore()
@@ -113,8 +123,13 @@
     total_slots = n_inst * slots
     wanted, counts = [], []
     for base in range(0, total_slots, 128):
+        block = (lane + base) // slots
+        other, place = block // n_chip, block % n_chip
+        dy = jnp.where(place < half - 1, place + 1, place + 2)
+        dy = jnp.where(place < n_near, dy, jnp.where(place == n_near, half, 0))
+        name = chip_at(dy, other) * slots + lane % slots
+        wanted.append(((borrow[0] == name) | (borrow[1] == name)).astype(F32))
         hit = [b == lane + base for b in borrow]
-        wanted.append((hit[0] | hit[1]).astype(F32))
         both = jnp.where(hit[0], counted[0], 0.0) + jnp.where(hit[1], counted[1], 0.0)
         counts.append(jnp.sum(both, axis=0, keepdims=True))
     wanted = jnp.concatenate(wanted, axis=1)[:, :total_slots].astype(BF16)
@@ -123,8 +138,7 @@
     asked = dot(wanted, q, ((0,), (0,))).astype(BF16)
     ask_out[...] = asked.reshape(n_inst, slots, 2 * HD)
     count_out[...] = counts
-    ask_in[n_inst - 1] = ask_out[me]
-    count_in[n_inst - 1] = counts
+    ask_in[n_near + 3] = ask_out[n_near + 1]
 
     pl.semaphore_wait(barrier, greeted)
 
@@ -133,8 +147,6 @@
             src_ref=src, dst_ref=dst, send_sem=send_sem.at[phase], recv_sem=recv_sem.at[phase], device_id=to
         ).start()
 
-    n_chip = n_inst // 2
-
     def to_chips(chips, act):
         for y in chips:
 
@@ -153,13 +165,23 @@
         part = ref.at[pl.ds(0, count)]
         pltpu.make_async_copy(part, part, send_sem.at[phase]).wait()
 
-    def ask(to):
-        place = (to - me - 1) % n_inst
-        send(ask_out.at[to], ask_in.at[place], 0, {"inst": to})
-        send(count_out, count_in.at[place], 1, {"inst": to})
-
-    to_chips(sorted(range(n_chip), key=lambda y: abs(y - n_chip // 2)), ask)
-
+    over = {"inst": sibling}
+    send(ask_out.at[pl.ds(n_chip, n_near)], ask_relay, 5, over)
+    send(count_out, count_relay, 6, over)
+    for other in range(2):
+        to = {"inst": chip_at(half, other)}
+        send(ask_out.at[other * n_chip + n_near], ask_in.at[n_near + other], 0, to)
+        send(count_out, count_in.at[n_near + other], 1, to)
+    send(ask_out.at[n_chip + n_near + 1], ask_in.at[n_near + 2], 0, over)
+    arrive(ask_relay, n_near, 5)
+    arrive(count_relay, 1, 6)
+    for p in range(n_near):
+        ask_out[p] = ask_out[p] + ask_relay[p]
+    count_sum[...] = counts + count_relay[...]
+    for p in far_first:
+        to = {"inst": chip_at(near[p])}
+        send(ask_out.at[p], ask_in.at[p], 0, to)
+        send(count_sum, count_in.at[p], 1, to)
     tell(0)
 
     row = lax.broadcasted_iota(I32, (2 * reqs, PAGE), 0) % reqs
@@ -203,13 +225,13 @@
     def spread(x):
         return jnp.concatenate([x * o for o in own], axis=1)
 
-    arrive(ask_in, n_inst - 1, 0)
-    arrive(count_in, n_inst - 1, 1)
+    arrive(ask_in, n_near + 3, 0)
+    arrive(count_in, n_near + 2, 1)
     q_lent = ask_in[0]
-    for k in range(1, n_inst):
+    for k in range(1, n_near + 4):
         q_lent = q_lent + ask_in[k]
     q_lent = by_head(q_lent)
-    count_row = jnp.sum(count_in[...], axis=0)
+    count_row = jnp.sum(count_in[...], axis=0) + counts + count_relay[...]
     wide = (slots, count_row.shape[1])
     mine = lax.broadcasted_iota(I32, wide, 1) == me * slots + lax.broadcasted_iota(I32, wide, 0)
     count_col = jnp.sum(jnp.where(mine, count_row, 0.0), axis=1, keepdims=True)
@@ -309,8 +331,10 @@
     result = result + jnp.sum(proj_in[...].astype(F32), axis=0)
     out_ref[...] = result.astype(out_ref.dtype)
 
-    sent(ask_in, n_inst - 1, 0)
-    sent(count_in, n_inst - 1, 1)
+    sent(ask_in, n_near + 3, 0)
+    sent(count_in, n_near + 2, 1)
+    sent(ask_relay, n_near, 5)
+    sent(count_relay, 1, 6)
     sent(part_in, n_inst - 1, 2)
     sent(stat_in, n_inst - 1, 3)
     sent(proj_in, n_tp - 1, 4)
@@ -336,9 +360,12 @@
             pltpu.SMEM(borrowed.shape[::-1], I32),
             pltpu.SMEM(lengths.shape, I32),
             pltpu.VMEM((n_inst, slots, 2 * HD), BF16),
-            pltpu.VMEM((n_inst, slots, 2 * HD), BF16),
+            pltpu.VMEM((n_inst // 2 + 2, slots, 2 * HD), BF16),
+            pltpu.VMEM((n_inst // 2 - 2, slots, 2 * HD), BF16),
             pltpu.VMEM((1, lanes), F32),
-            pltpu.VMEM((n_inst, 1, lanes), F32),
+            pltpu.VMEM((n_inst // 2, 1, lanes), F32),
+            pltpu.VMEM((1, lanes), F32),
+            pltpu.VMEM((1, lanes), F32),
             pltpu.VMEM((slots, 2 * HD), BF16),
             pltpu.VMEM((n_inst, slots, 2 * HD), BF16),
             pltpu.VMEM((1, 128), F32),
@@ -347,8 +374,8 @@
             pltpu.VMEM((n_tp - 1, reqs, cols), BF16),
             pltpu.VMEM((slots * HD, PAGE), BF16),
             pltpu.SemaphoreType.DMA((7,)),
-            pltpu.SemaphoreType.DMA((5,)),
-            pltpu.SemaphoreType.DMA((5,)),
+            pltpu.SemaphoreType.DMA((7,)),
+            pltpu.SemaphoreType.DMA((7,)),
             pltpu.SemaphoreType.REGULAR((3,)),
         ],
         compiler_params=pltpu.CompilerParams(

time: 32.9 us -> 32 us (0.973); the launches traced: 32.4 us -> 31.9 us
  Pallas kernels: 31.8 us -> 31.3 us
    pallas_call x1, Pallas kernels: 31.8 us -> 31.3 us  [shards(): pl.pallas_call(functools.partial(fused, n_inst, n_tp // nx, nx), out_shap...]
where the time goes in v4:
time: 32 us; the launch traced here: 31.9 us
  Pallas kernels  31.3 us (98%)
  local copies, waits for them, and re-layouts  0.6 us (2%)
    pallas_call x1, Pallas kernels, shards(): pl.pallas_call(functools.partial(fused, n_inst, n_tp // nx, nx), out_shap...  31.3 us

profile of v4, /device:TPU:1, one launch (start us, length us, event | category | flops | bytes accessed | tf_op | source)
XLA Modules:
  0.0 31.9 jit_solution(4904972999106493038)
XLA Ops:
  0.0 31.3 %shard_map.73 = bf16[16,128]{1,0:T(8,128)(2,1)S(1)} custom-call(bf16[16,256]{1,0:T(8,128)(2,1)} %q_hbm.1, bf16[24,1,128,256]{3,2,1,0:T(8,128)(2,1)} %home_hbm.1, bf16[16,1,128,256]{3,2,1,0:T(8,128)(2,1)} %lent_hbm.1, s32[2,16]{1,0:T(2,128)} %bitcast.2, s32[2,16]{1,0:T(2,128)} %bitcast.3, s32[16]{0:T(128)} %lengths_hbm.1, bf16[256,4096]{1,0:T(8,128)(2,1)} %weight_hbm.1), custom_call_target="tpu_custom_call" | custom-call | tf_op jit(solution)/shard_map/pallas_call | solution.py:349
  31.3 0.6 %copy.9 = bf16[16,128]{1,0:T(8,128)(2,1)} copy(bf16[16,128]{1,0:T(8,128)(2,1)S(1)} %shard_map.73) | data formatting | bytes 8192

commit v5 on v4

--- a/solution.py
+++ b/solution.py
@@ -166,12 +166,12 @@
         pltpu.make_async_copy(part, part, send_sem.at[phase]).wait()
 
     over = {"inst": sibling}
-    send(ask_out.at[pl.ds(n_chip, n_near)], ask_relay, 5, over)
-    send(count_out, count_relay, 6, over)
     for other in range(2):
         to = {"inst": chip_at(half, other)}
         send(ask_out.at[other * n_chip + n_near], ask_in.at[n_near + other], 0, to)
         send(count_out, count_in.at[n_near + other], 1, to)
+    send(ask_out.at[pl.ds(n_chip, n_near)], ask_relay, 5, over)
+    send(count_out, count_relay, 6, over)
     send(ask_out.at[n_chip + n_near + 1], ask_in.at[n_near + 2], 0, over)
     arrive(ask_relay, n_near, 5)
     arrive(count_relay, 1, 6)
@@ -276,11 +276,11 @@
 
     arrive(stat_in, n_inst - 1, 3)
     left_over = stat_in[...].reshape(n_inst, 128)
-    found = jnp.zeros(two.shape, F32)
+    pieces = []
     for _ in range(3):
-        piece = left_over.astype(BF16)
-        found = found + dot(lender, piece)
-        left_over = left_over - piece.astype(F32)
+        pieces.append(left_over.astype(BF16))
+        left_over = left_over - pieces[-1].astype(F32)
+    found = dot(jnp.concatenate([lender] * 3, axis=1), jnp.concatenate(pieces, axis=0))
     present = two[:, :1] >= 0
 
     def pick(kind, absent):
@@ -326,11 +326,6 @@
 
     for d in range(1, nx):
         hand_over(my_z, (my_x + d) % nx)
-    result = proj_out[tp].astype(F32)
-    arrive(proj_in, n_tp - 1, 4)
-    result = result + jnp.sum(proj_in[...].astype(F32), axis=0)
-    out_ref[...] = result.astype(out_ref.dtype)
-
     sent(ask_in, n_near + 3, 0)
     sent(count_in, n_near + 2, 1)
     sent(ask_relay, n_near, 5)
@@ -338,6 +333,11 @@
     sent(part_in, n_inst - 1, 2)
     sent(stat_in, n_inst - 1, 3)
     sent(proj_in, n_tp - 1, 4)
+    arrive(proj_in, n_tp - 1, 4)
+    terms = [proj_out[tp].astype(F32)] + [proj_in[k].astype(F32) for k in range(n_tp - 1)]
+    while len(terms) > 1:
+        terms = [sum(terms[k : k + 2]) for k in range(0, len(terms), 2)]
+    out_ref[...] = terms[0].astype(out_ref.dtype)
 
 
 def shards(nx, queries, home_kv, lent_kv, page_table, borrowed, lengths, out_weight):

time: 32 us -> 32 us (level)
  no operation moved by 1% of the time
where the time goes in v5:
time: 32 us; the launch traced here: 31.9 us
  Pallas kernels  31.3 us (98%)
  local copies, waits for them, and re-layouts  0.6 us (2%)
    pallas_call x1, Pallas kernels, shards(): pl.pallas_call(functools.partial(fused, n_inst, n_tp // nx, nx), out_shap...  31.3 us

profile of v5, /device:TPU:1, one launch (start us, length us, event | category | flops | bytes accessed | tf_op | source)
XLA Modules:
  0.0 31.9 jit_solution(17547555024532757216)
XLA Ops:
  0.0 31.3 %shard_map.73 = bf16[16,128]{1,0:T(8,128)(2,1)S(1)} custom-call(bf16[16,256]{1,0:T(8,128)(2,1)} %q_hbm.1, bf16[24,1,128,256]{3,2,1,0:T(8,128)(2,1)} %home_hbm.1, bf16[16,1,128,256]{3,2,1,0:T(8,128)(2,1)} %lent_hbm.1, s32[2,16]{1,0:T(2,128)} %bitcast.2, s32[2,16]{1,0:T(2,128)} %bitcast.3, s32[16]{0:T(128)} %lengths_hbm.1, bf16[256,4096]{1,0:T(8,128)(2,1)} %weight_hbm.1), custom_call_target="tpu_custom_call" | custom-call | tf_op jit(solution)/shard_map/pallas_call | solution.py:349
  31.3 0.6 %copy.9 = bf16[16,128]{1,0:T(8,128)(2,1)} copy(bf16[16,128]{1,0:T(8,128)(2,1)S(1)} %shard_map.73) | data formatting | bytes 8192

commit v6 on v5

--- a/solution.py
+++ b/solution.py
@@ -183,34 +183,6 @@
         send(ask_out.at[p], ask_in.at[p], 0, to)
         send(count_sum, count_in.at[p], 1, to)
     tell(0)
-
-    row = lax.broadcasted_iota(I32, (2 * reqs, PAGE), 0) % reqs
-    token = lax.broadcasted_iota(I32, (2 * reqs, PAGE), 1)
-    q2 = by_head(q)
-    loads[4].wait()
-    scores = [jnp.zeros((2 * reqs, PAGE), F32) for _ in range(RANKS)]
-    usable = [jnp.zeros((2 * reqs, PAGE), I32) for _ in range(RANKS)]
-    for r in range(reqs):
-        for j in range(RANKS):
-            page = jnp.maximum(table[r][j], 0)
-            s = dot(q2, home_v[page, 0, :, :HD], ((1,), (1,)))
-            scores[j] = jnp.where(row == r, s, scores[j])
-            here = jnp.where(table[r][j] >= 0, length[r] - PAGE * j, 0)
-            usable[j] = jnp.where(row == r, here, usable[j])
-    usable = [token < u for u in usable]
-    scores = [jnp.where(u, s * scale, SENTINEL) for u, s in zip(usable, scores)]
-    home_max = jnp.max(jnp.maximum(scores[0], scores[1]), axis=1, keepdims=True)
-    home_w = [
-        jnp.where(u, jnp.exp(s - home_max), 0.0).astype(BF16) for u, s in zip(usable, scores)
-    ]
-    home_total = sum(jnp.sum(w.astype(F32), axis=1, keepdims=True) for w in home_w)
-    home_sum = jnp.zeros((2 * reqs, HD), F32)
-    for r in range(reqs):
-        o = 0.0
-        for j in range(RANKS):
-            page = jnp.maximum(table[r][j], 0)
-            o = o + dot(home_w[j], home_v[page, 0, :, HD:])
-        home_sum = jnp.where(row == r, o, home_sum)
 
     told(0)
     tell(1)
@@ -261,6 +233,34 @@
 
     told(1)
     tell(2)
+
+    row = lax.broadcasted_iota(I32, (2 * reqs, PAGE), 0) % reqs
+    token = lax.broadcasted_iota(I32, (2 * reqs, PAGE), 1)
+    q2 = by_head(q)
+    loads[4].wait()
+    scores = [jnp.zeros((2 * reqs, PAGE), F32) for _ in range(RANKS)]
+    usable = [jnp.zeros((2 * reqs, PAGE), I32) for _ in range(RANKS)]
+    for r in range(reqs):
+        for j in range(RANKS):
+            page = jnp.maximum(table[r][j], 0)
+            s = dot(q2, home_v[page, 0, :, :HD], ((1,), (1,)))
+            scores[j] = jnp.where(row == r, s, scores[j])
+            here = jnp.where(table[r][j] >= 0, length[r] - PAGE * j, 0)
+            usable[j] = jnp.where(row == r, here, usable[j])
+    usable = [token < u for u in usable]
+    scores = [jnp.where(u, s * scale, SENTINEL) for u, s in zip(usable, scores)]
+    home_max = jnp.max(jnp.maximum(scores[0], scores[1]), axis=1, keepdims=True)
+    home_w = [
+        jnp.where(u, jnp.exp(s - home_max), 0.0).astype(BF16) for u, s in zip(usable, scores)
+    ]
+    home_total = sum(jnp.sum(w.astype(F32), axis=1, keepdims=True) for w in home_w)
+    home_sum = jnp.zeros((2 * reqs, HD), F32)
+    for r in range(reqs):
+        o = 0.0
+        for j in range(RANKS):
+            page = jnp.maximum(table[r][j], 0)
+            o = o + dot(home_w[j], home_v[page, 0, :, HD:])
+        home_sum = jnp.where(row == r, o, home_sum)
 
     two = jnp.concatenate(borrow, axis=0)
     gather = []

time: 32 us -> 32.1 us (level)
  no operation moved by 1% of the time
where the time goes in v6:
time: 32.1 us; the launch traced here: 32 us
  Pallas kernels  31.4 us (98%)
  local copies, waits for them, and re-layouts  0.6 us (2%)
    pallas_call x1, Pallas kernels, shards(): pl.pallas_call(functools.partial(fused, n_inst, n_tp // nx, nx), out_shap...  31.4 us

profile of v6, /device:TPU:1, one launch (start us, length us, event | category | flops | bytes accessed | tf_op | source)
XLA Modules:
  0.0 32.0 jit_solution(6513305943375253355)
XLA Ops:
  0.0 31.4 %shard_map.73 = bf16[16,128]{1,0:T(8,128)(2,1)S(1)} custom-call(bf16[16,256]{1,0:T(8,128)(2,1)} %q_hbm.1, bf16[24,1,128,256]{3,2,1,0:T(8,128)(2,1)} %home_hbm.1, bf16[16,1,128,256]{3,2,1,0:T(8,128)(2,1)} %lent_hbm.1, s32[2,16]{1,0:T(2,128)} %bitcast.2, s32[2,16]{1,0:T(2,128)} %bitcast.3, s32[16]{0:T(128)} %lengths_hbm.1, bf16[256,4096]{1,0:T(8,128)(2,1)} %weight_hbm.1), custom_call_target="tpu_custom_call" | custom-call | tf_op jit(solution)/shard_map/pallas_call | solution.py:349
  31.4 0.6 %copy.9 = bf16[16,128]{1,0:T(8,128)(2,1)} copy(bf16[16,128]{1,0:T(8,128)(2,1)S(1)} %shard_map.73) | data formatting | bytes 8192
